TPU v7x, 32 devices: a whole 2x2x4 slice. The times are simulated.
32 devices in a mesh: gx: 4 (over x, core), gy: 2 (over y), gz: 4 (over z).
Axes of the slice: x: 2, y: 2, z: 4, core: 2. Of those that a mesh axis runs over, the one named last changes fastest.
Arguments:
- phase: int32 [256, 16, 512], P('gx', 'gy', 'gz'), may hold values from 0 to 2
- perm_scale: float32 [256, 16, 512], P('gx', 'gy', 'gz'), may hold values from 0.5 to 2
- magnetization: bfloat16 [3, 256, 16, 512], P(None, 'gx', 'gy', 'gz'), may hold values from -4 to 4
- stiffness: float32 [256, 16, 512], P(('gx', 'gy'), None, 'gz'), may hold values from 0.5 to 4
Outputs:
- strain: bfloat16 [6, 256, 16, 512], P(None, 'gx', 'gy', 'gz')
All inputs are finite; a program needn't handle non-finite values.
Results may differ from a plain program's by a relative error of at most 0.001.
The roundings to bfloat16 on the way count: a program that leaves them out, or rounds other values in their place, can miss the bound.
Values may be sent and summed in bfloat16 or wider, within the bound.
A program may use at most 64 MiB of HBM per device.

v0:
```python
import math
import jax
import jax.numpy as jnp
from jax import lax
from jax.sharding import PartitionSpec as P

SWEEPS = 3
STRAIN_PAIRS = ((0, 0), (1, 1), (2, 2), (0, 1), (1, 2), (0, 2))
MAGNETO = 4.0


def padded_2(value, sides, width):
    for axis, dim in sides:
        devices, length = (lax.axis_size(axis), value.shape[dim])
        up = [(i, (i + 1) % devices) for i in range(devices - 1)]
        down = [(j, i) for i, j in up]
        last = lax.slice_in_dim(value, length - width, length, axis=dim)
        leading = lax.slice_in_dim(value, 0, width, axis=dim)
        before = lax.ppermute(last, axis, up)
        after = lax.ppermute(leading, axis, down)
        value = jnp.concatenate([before, value, after], axis=dim)
    return value


def chebyshev_weights(middle, radius, count):
    return [
        1.0 / (middle + radius * math.cos((2 * counter + 1) * math.pi / (2 * count)))
        for counter in range(count)
    ]


def unit_offset(dimension, sign):
    offsets = [0, 0, 0]
    offsets[dimension] = sign
    return offsets


def window(padded, offsets):
    shape = padded.shape[-3:]
    selection = tuple(
        (slice(1 + moved, extent - 1 + moved) for moved, extent in zip(offsets, shape))
    )
    leading = tuple((slice(None) for counter in range(padded.ndim - 3)))
    return padded[leading + selection]


def central(padded, dimension):
    return (
        window(padded, unit_offset(dimension, 1)) - window(padded, unit_offset(dimension, -1))
    ) * 0.5


def neighbours(padded):
    total = window(padded, unit_offset(0, 1)) + window(padded, unit_offset(0, -1))
    for dimension in (1, 2):
        total = (
            total
            + window(padded, unit_offset(dimension, 1))
            + window(padded, unit_offset(dimension, -1))
        )
    return total


def magnet_force(moments_pad, potential_pad):
    total = [moments_pad[dimension] - central(potential_pad, dimension) for dimension in range(3)]
    inner = moments_pad[0] * total[0] + moments_pad[1] * total[1] + moments_pad[2] * total[2]
    stress = {}
    for first, second in STRAIN_PAIRS:
        value = 0.5 * (moments_pad[first] * total[second] + moments_pad[second] * total[first])
        if first == second:
            value = value - inner / 3.0
        stress[first, second] = MAGNETO * value
        stress[second, first] = stress[first, second]
    force = []
    for first in range(3):
        acc = central(stress[first, 0], 0)
        for second in (1, 2):
            acc = acc + central(stress[first, second], second)
        force.append(acc)
    return jnp.stack(force)


def navier(padded):
    result = []
    for first in range(3):
        center = window(padded[first], [0, 0, 0])
        value = 6.0 * center - neighbours(padded[first])
        second_diff = (
            window(padded[first], unit_offset(first, 1))
            - 2.0 * center
            + window(padded[first], unit_offset(first, -1))
        )
        for second in range(3):
            if second != first:
                plus_plus = [0, 0, 0]
                plus_plus[first] = 1
                plus_plus[second] = 1
                plus_minus = [0, 0, 0]
                plus_minus[first] = 1
                plus_minus[second] = -1
                minus_plus = [0, 0, 0]
                minus_plus[first] = -1
                minus_plus[second] = 1
                minus_minus = [0, 0, 0]
                minus_minus[first] = -1
                minus_minus[second] = -1
                second_diff = second_diff + 0.25 * (
                    window(padded[second], plus_plus)
                    - window(padded[second], plus_minus)
                    - window(padded[second], minus_plus)
                    + window(padded[second], minus_minus)
                )
        result.append(value - second_diff)
    return jnp.stack(result)


def strain_from(padded):
    result = []
    for first, second in STRAIN_PAIRS:
        result.append(0.5 * (central(padded[second], first) + central(padded[first], second)))
    return jnp.stack(result)


def potential_rim(field):
    return padded_2(field, (("gx", 0), ("gy", 1), ("gz", 2)), 2)


def elastic_solve(load, modulus, pad_field):
    elastic_weights = chebyshev_weights(1.3, 1.2, SWEEPS)
    elastic_diag = 8.0 * modulus
    displacement = elastic_weights[0] * load / elastic_diag
    for counter in range(1, SWEEPS):
        padded = pad_field(displacement)
        displacement = (
            displacement
            + elastic_weights[counter] * (load - modulus * navier(padded)) / elastic_diag
        )
    return displacement


def per_device(phase, perm_scale, magnetization, stiffness):
    magnetic = phase == 0
    permeability = (
        jnp.where(magnetic, 4.0, jnp.where(phase == 1, 1.5, 1.0)).astype(jnp.float32) * perm_scale
    )
    moments = magnetization * magnetic.astype(jnp.bfloat16)[None]
    moments_pad = padded_2(moments, (("gx", 1), ("gy", 2), ("gz", 3)), 1).astype(jnp.float32)
    source = -(central(moments_pad[0], 0) + central(moments_pad[1], 1) + central(moments_pad[2], 2))
    weights = chebyshev_weights(1.0, 0.9, SWEEPS)
    diagonal = 6.0 * permeability
    potential = weights[0] * source / diagonal
    for counter in range(1, SWEEPS):
        padded = potential_rim(potential)[1:-1, 1:-1, 1:-1]
        potential = (
            potential
            + weights[counter]
            * (source - permeability * (6.0 * potential - neighbours(padded)))
            / diagonal
        )
    force = magnet_force(moments_pad, potential_rim(potential)).astype(jnp.bfloat16)
    load = lax.all_to_all(force, "gy", split_axis=1, concat_axis=2, tiled=True).astype(jnp.float32)

    def pad_slab(field):
        rimmed = padded_2(field, ((("gx", "gy"), 1), ("gz", 3)), 1)
        return jnp.pad(rimmed, ((0, 0), (0, 0), (1, 1), (0, 0)))

    displacement = elastic_solve(load, stiffness, pad_slab)
    strain = strain_from(pad_slab(displacement)).astype(jnp.bfloat16)
    return lax.all_to_all(strain, "gy", split_axis=2, concat_axis=1, tiled=True)


def solution(mesh):
    placed = (
        P("gx", "gy", "gz"),
        P("gx", "gy", "gz"),
        P(None, "gx", "gy", "gz"),
        P(("gx", "gy"), None, "gz"),
    )
    return jax.shard_map(
        per_device, mesh=mesh, in_specs=placed, out_specs=P(None, "gx", "gy", "gz"), check_vma=False
    )
```

profile of v0, /device:TPU:0, one launch (start us, length us, event | category | flops | bytes accessed | tf_op | source)
XLA Modules:
  0.0 224.6 jit_solution(4618047857174763802)
XLA Ops:
  2.4 2.4 %collective-permute-start = (bf16[3,1,8,128]{3,2,1,0:T(8,128)(2,1)S(1)}, bf16[3,1,8,128]{3,2,1,0:T(8,128)(2,1)S(1)}, u32[]{:S(2)}, u32[]{:S(2)}) collective-permute-start(bf16[3,1,8,128]{3,2,1,0:T(8,128)(2,1)S(1)} %get-tuple-element.66), channel_id=1, source_target_pairs={{0,8},{8,16},{16,24},{1,9},{9,17},{17,25},{2,10},{10,18},{18,26},{... | collective-permute-start | bytes 18440 | tf_op jit(solution)/shard_map/ppermute | solution.py:19
  6.1 3.9 %collective-permute-done.1 = bf16[3,1,8,128]{3,2,1,0:T(8,128)(2,1)S(1)} collective-permute-done((bf16[3,1,8,128]{3,2,1,0:T(8,128)(2,1)S(1)}, bf16[3,1,8,128]{3,2,1,0:T(8,128)(2,1)S(1)}, u32[]{:S(2)}, u32[]{:S(2)}) %collective-permute-start.1) | collective-permute-done | bytes 6176 | tf_op jit(solution)/shard_map/ppermute | solution.py:20
  10.5 3.4 %collective-permute-start.2 = (bf16[3,66,1,128]{1,3,2,0:T(8,128)(2,1)S(1)}, bf16[3,66,1,128]{1,3,2,0:T(8,128)(2,1)S(1)}, u32[]{:S(2)}, u32[]{:S(2)}) collective-permute-start(bf16[3,66,1,128]{1,3,2,0:T(8,128)(2,1)S(1)} %get-tuple-element.55), channel_id=1, source_target_pairs={{0,4},{1,5},{2,6},{3,7},{8,12},{9,13},{10,14},{11,15},{16,20},{17,... | collective-permute-start | bytes 152072 | tf_op jit(solution)/shard_map/ppermute | solution.py:19
  16.1 4.3 %collective-permute-done.3 = bf16[3,66,1,128]{1,3,2,0:T(8,128)(2,1)S(1)} collective-permute-done((bf16[3,66,1,128]{1,3,2,0:T(8,128)(2,1)S(1)}, bf16[3,66,1,128]{1,3,2,0:T(8,128)(2,1)S(1)}, u32[]{:S(2)}, u32[]{:S(2)}) %collective-permute-start.3) | collective-permute-done | bytes 50720 | tf_op jit(solution)/shard_map/ppermute | solution.py:20
  20.5 3.5 %collective-permute-start.4 = (bf16[3,66,10,1]{1,0,3,2:T(4,128)(2,1)S(1)}, bf16[3,66,10,1]{1,0,3,2:T(4,128)(2,1)S(1)}, u32[]{:S(2)}, u32[]{:S(2)}) collective-permute-start(bf16[3,66,10,1]{1,0,3,2:T(4,128)(2,1)S(1)} %copy.93), channel_id=1, source_target_pairs={{0,1},{1,2},{2,3},{4,5},{5,6},{6,7},{8,9},{9,10},{10,11},{12,13},{... | collective-permute-start | bytes 11888 | tf_op jit(solution)/shard_map/ppermute | solution.py:19
  25.6 4.0 %collective-permute-done.5 = bf16[3,66,10,1]{1,0,3,2:T(4,128)(2,1)S(1)} collective-permute-done((bf16[3,66,10,1]{1,0,3,2:T(4,128)(2,1)S(1)}, bf16[3,66,10,1]{1,0,3,2:T(4,128)(2,1)S(1)}, u32[]{:S(2)}, u32[]{:S(2)}) %collective-permute-start.5) | collective-permute-done | bytes 3992 | tf_op jit(solution)/shard_map/ppermute | solution.py:20
  32.3 3.1 %collective-permute-start.7 = (f32[2,8,128]{0,2,1:T(8,128)S(1)}, f32[2,8,128]{0,2,1:T(8,128)S(1)}, u32[]{:S(2)}, u32[]{:S(2)}) collective-permute-start(f32[2,8,128]{0,2,1:T(8,128)S(1)} %get-tuple-element.64), channel_id=1, source_target_pairs={{0,8},{8,16},{16,24},{1,9},{9,17},{17,25},{2,10},{10,18},{18,26},{... | collective-permute-start | bytes 24584 | tf_op jit(solution)/shard_map/ppermute | solution.py:19
  38.4 4.6 %collective-permute-start.9 = (f32[68,2,128]{0,2,1:T(8,128)S(1)}, f32[68,2,128]{0,2,1:T(8,128)S(1)}, u32[]{:S(2)}, u32[]{:S(2)}) collective-permute-start(f32[68,2,128]{0,2,1:T(8,128)S(1)} %get-tuple-element.39), channel_id=1, source_target_pairs={{0,4},{1,5},{2,6},{3,7},{8,12},{9,13},{10,14},{11,15},{16,20},{17,... | collective-permute-start | bytes 208904 | tf_op jit(solution)/shard_map/ppermute | solution.py:19
  46.9 4.5 %collective-permute-start.11 = (f32[68,12,2]{0,2,1:T(2,128)S(1)}, f32[68,12,2]{0,2,1:T(2,128)S(1)}, u32[]{:S(2)}, u32[]{:S(2)}) collective-permute-start(f32[68,12,2]{0,2,1:T(2,128)S(1)} %get-tuple-element.34), channel_id=1, source_target_pairs={{0,1},{1,2},{2,3},{4,5},{5,6},{6,7},{8,9},{9,10},{10,11},{12,13},{... | collective-permute-start | bytes 19592 | tf_op jit(solution)/shard_map/ppermute | solution.py:19
  56.0 6.8 %collective-permute-start.13 = (f32[2,8,128]{0,2,1:T(8,128)S(1)}, f32[2,8,128]{0,2,1:T(8,128)S(1)}, u32[]{:S(2)}, u32[]{:S(2)}) collective-permute-start(f32[2,8,128]{0,2,1:T(8,128)S(1)} %get-tuple-element.62), channel_id=1, source_target_pairs={{0,8},{8,16},{16,24},{1,9},{9,17},{17,25},{2,10},{10,18},{18,26},{... | collective-permute-start | bytes 24584 | tf_op jit(solution)/shard_map/ppermute | solution.py:19
  65.8 4.6 %collective-permute-start.15 = (f32[68,2,128]{0,2,1:T(8,128)S(1)}, f32[68,2,128]{0,2,1:T(8,128)S(1)}, u32[]{:S(2)}, u32[]{:S(2)}) collective-permute-start(f32[68,2,128]{0,2,1:T(8,128)S(1)} %get-tuple-element.37), channel_id=1, source_target_pairs={{0,4},{1,5},{2,6},{3,7},{8,12},{9,13},{10,14},{11,15},{16,20},{17,... | collective-permute-start | bytes 208904 | tf_op jit(solution)/shard_map/ppermute | solution.py:19
  74.3 4.5 %collective-permute-start.17 = (f32[68,12,2]{0,2,1:T(2,128)S(1)}, f32[68,12,2]{0,2,1:T(2,128)S(1)}, u32[]{:S(2)}, u32[]{:S(2)}) collective-permute-start(f32[68,12,2]{0,2,1:T(2,128)S(1)} %get-tuple-element.32), channel_id=1, source_target_pairs={{0,1},{1,2},{2,3},{4,5},{5,6},{6,7},{8,9},{9,10},{10,11},{12,13},{... | collective-permute-start | bytes 19592 | tf_op jit(solution)/shard_map/ppermute | solution.py:19
  82.1 9.6 %collective-permute-start.18 = (f32[2,8,128]{0,2,1:T(8,128)S(1)}, f32[2,8,128]{0,2,1:T(8,128)S(1)}, u32[]{:S(2)}, u32[]{:S(2)}) collective-permute-start(f32[2,8,128]{0,2,1:T(8,128)S(1)} %get-tuple-element.60), channel_id=1, source_target_pairs={{0,8},{8,16},{16,24},{1,9},{9,17},{17,25},{2,10},{10,18},{18,26},{... | collective-permute-start | bytes 24584 | tf_op jit(solution)/shard_map/ppermute | solution.py:19
  93.3 6.2 %collective-permute-done.19 = f32[2,8,128]{0,2,1:T(8,128)S(1)} collective-permute-done((f32[2,8,128]{0,2,1:T(8,128)S(1)}, f32[2,8,128]{0,2,1:T(8,128)S(1)}, u32[]{:S(2)}, u32[]{:S(2)}) %collective-permute-start.19) | collective-permute-done | bytes 8224 | tf_op jit(solution)/shard_map/ppermute | solution.py:20
  99.6 4.4 %collective-permute-start.20 = (f32[68,2,128]{0,2,1:T(8,128)S(1)}, f32[68,2,128]{0,2,1:T(8,128)S(1)}, u32[]{:S(2)}, u32[]{:S(2)}) collective-permute-start(f32[68,2,128]{0,2,1:T(8,128)S(1)} %get-tuple-element.35), channel_id=1, source_target_pairs={{0,4},{1,5},{2,6},{3,7},{8,12},{9,13},{10,14},{11,15},{16,20},{17,... | collective-permute-start | bytes 208904 | tf_op jit(solution)/shard_map/ppermute | solution.py:19
  106.5 4.4 %collective-permute-done.21 = f32[68,2,128]{0,2,1:T(8,128)S(1)} collective-permute-done((f32[68,2,128]{0,2,1:T(8,128)S(1)}, f32[68,2,128]{0,2,1:T(8,128)S(1)}, u32[]{:S(2)}, u32[]{:S(2)}) %collective-permute-start.21) | collective-permute-done | bytes 69664 | tf_op jit(solution)/shard_map/ppermute | solution.py:20
  111.0 4.2 %collective-permute-start.22 = (f32[68,12,2]{0,2,1:T(2,128)S(1)}, f32[68,12,2]{0,2,1:T(2,128)S(1)}, u32[]{:S(2)}, u32[]{:S(2)}) collective-permute-start(f32[68,12,2]{0,2,1:T(2,128)S(1)} %get-tuple-element.29), channel_id=1, source_target_pairs={{0,1},{1,2},{2,3},{4,5},{5,6},{6,7},{8,9},{9,10},{10,11},{12,13},{... | collective-permute-start | bytes 19592 | tf_op jit(solution)/shard_map/ppermute | solution.py:19
  116.7 4.1 %collective-permute-done.23 = f32[68,12,2]{0,2,1:T(2,128)S(1)} collective-permute-done((f32[68,12,2]{0,2,1:T(2,128)S(1)}, f32[68,12,2]{0,2,1:T(2,128)S(1)}, u32[]{:S(2)}, u32[]{:S(2)}) %collective-permute-start.23) | collective-permute-done | bytes 6560 | tf_op jit(solution)/shard_map/ppermute | solution.py:20
  126.6 3.5 %all-to-all-start = ((bf16[3,64,8,128]{3,2,0,1:T(8,128)(2,1)}), bf16[3,64,8,128]{3,2,0,1:T(8,128)(2,1)S(1)}, u32[]{:S(2)}, u32[]{:S(2)}) async-start(bf16[3,64,8,128]{3,2,0,1:T(8,128)(2,1)} %copy.99), calls=%async_computation | async-start | bytes 786432 | tf_op jit(solution)/shard_map/all_to_all | solution.py:161
  130.1 5.8 %all-to-all-done = bf16[3,64,8,128]{3,2,0,1:T(8,128)(2,1)S(1)} async-done(((bf16[3,64,8,128]{3,2,0,1:T(8,128)(2,1)}), bf16[3,64,8,128]{3,2,0,1:T(8,128)(2,1)S(1)}, u32[]{:S(2)}, u32[]{:S(2)}) %all-to-all-start) | async-done | bytes 393248 | tf_op jit(solution)/shard_map/all_to_all | solution.py:161
  139.6 7.3 %collective-permute-done.25 = f32[3,1,16,128]{3,2,1,0:T(8,128)S(1)} collective-permute-done((f32[3,1,16,128]{3,2,1,0:T(8,128)S(1)}, f32[3,1,16,128]{3,2,1,0:T(8,128)S(1)}, u32[]{:S(2)}, u32[]{:S(2)}) %collective-permute-start.25) | collective-permute-done | bytes 24608 | tf_op jit(solution)/shard_map/ppermute | solution.py:20
  147.7 3.6 %collective-permute-start.26 = (f32[3,34,16,1]{1,2,3,0:T(8,128)S(1)}, f32[3,34,16,1]{1,2,3,0:T(8,128)S(1)}, u32[]{:S(2)}, u32[]{:S(2)}) collective-permute-start(f32[3,34,16,1]{1,2,3,0:T(8,128)S(1)} %copy.102), channel_id=1, source_target_pairs={{0,1},{1,2},{2,3},{4,5},{5,6},{6,7},{8,9},{9,10},{10,11},{12,13},{... | collective-permute-start | bytes 19592 | tf_op jit(solution)/shard_map/ppermute | solution.py:19
  153.6 3.9 %collective-permute-done.27 = f32[3,34,16,1]{1,2,3,0:T(8,128)S(1)} collective-permute-done((f32[3,34,16,1]{1,2,3,0:T(8,128)S(1)}, f32[3,34,16,1]{1,2,3,0:T(8,128)S(1)}, u32[]{:S(2)}, u32[]{:S(2)}) %collective-permute-start.27) | collective-permute-done | bytes 6560 | tf_op jit(solution)/shard_map/ppermute | solution.py:20
  162.5 3.3 %collective-permute-start.28 = (f32[3,1,16,128]{3,2,1,0:T(8,128)S(1)}, f32[3,1,16,128]{3,2,1,0:T(8,128)S(1)}, u32[]{:S(2)}, u32[]{:S(2)}) collective-permute-start(f32[3,1,16,128]{3,2,1,0:T(8,128)S(1)} %get-tuple-element.51), channel_id=1, source_target_pairs={{0,4},{4,8},{8,12},{12,16},{16,20},{20,24},{24,28},{1,5},{5,9},{9,... | collective-permute-start | bytes 73736 | tf_op jit(solution)/shard_map/ppermute | solution.py:19
  167.3 4.2 %collective-permute-done.29 = f32[3,1,16,128]{3,2,1,0:T(8,128)S(1)} collective-permute-done((f32[3,1,16,128]{3,2,1,0:T(8,128)S(1)}, f32[3,1,16,128]{3,2,1,0:T(8,128)S(1)}, u32[]{:S(2)}, u32[]{:S(2)}) %collective-permute-start.29) | collective-permute-done | bytes 24608 | tf_op jit(solution)/shard_map/ppermute | solution.py:20
  172.3 3.5 %collective-permute-start.30 = (f32[3,34,16,1]{1,2,3,0:T(8,128)S(1)}, f32[3,34,16,1]{1,2,3,0:T(8,128)S(1)}, u32[]{:S(2)}, u32[]{:S(2)}) collective-permute-start(f32[3,34,16,1]{1,2,3,0:T(8,128)S(1)} %copy.106), channel_id=1, source_target_pairs={{0,1},{1,2},{2,3},{4,5},{5,6},{6,7},{8,9},{9,10},{10,11},{12,13},{... | collective-permute-start | bytes 19592 | tf_op jit(solution)/shard_map/ppermute | solution.py:19
  178.1 3.9 %collective-permute-done.31 = f32[3,34,16,1]{1,2,3,0:T(8,128)S(1)} collective-permute-done((f32[3,34,16,1]{1,2,3,0:T(8,128)S(1)}, f32[3,34,16,1]{1,2,3,0:T(8,128)S(1)}, u32[]{:S(2)}, u32[]{:S(2)}) %collective-permute-start.31) | collective-permute-done | bytes 6560 | tf_op jit(solution)/shard_map/ppermute | solution.py:20
  187.1 4.1 %collective-permute-start.32 = (f32[3,1,16,128]{3,2,1,0:T(8,128)S(1)}, f32[3,1,16,128]{3,2,1,0:T(8,128)S(1)}, u32[]{:S(2)}, u32[]{:S(2)}) collective-permute-start(f32[3,1,16,128]{3,2,1,0:T(8,128)S(1)} %get-tuple-element.49), channel_id=1, source_target_pairs={{0,4},{4,8},{8,12},{12,16},{16,20},{20,24},{24,28},{1,5},{5,9},{9,... | collective-permute-start | bytes 73736 | tf_op jit(solution)/shard_map/ppermute | solution.py:19
  192.7 4.4 %collective-permute-done.33 = f32[3,1,16,128]{3,2,1,0:T(8,128)S(1)} collective-permute-done((f32[3,1,16,128]{3,2,1,0:T(8,128)S(1)}, f32[3,1,16,128]{3,2,1,0:T(8,128)S(1)}, u32[]{:S(2)}, u32[]{:S(2)}) %collective-permute-start.33) | collective-permute-done | bytes 24608 | tf_op jit(solution)/shard_map/ppermute | solution.py:20
  197.9 2.2 collective-permute-start.34
  202.3 3.9 %collective-permute-done.35 = f32[3,34,16,1]{1,2,3,0:T(8,128)S(1)} collective-permute-done((f32[3,34,16,1]{1,2,3,0:T(8,128)S(1)}, f32[3,34,16,1]{1,2,3,0:T(8,128)S(1)}, u32[]{:S(2)}, u32[]{:S(2)}) %collective-permute-start.35) | collective-permute-done | bytes 6560 | tf_op jit(solution)/shard_map/ppermute | solution.py:20
  210.0 13.2 %all_to_all.27 = bf16[6,32,16,128]{3,1,0,2:T(8,128)(2,1)S(1)} all-to-all(bf16[6,32,16,128]{3,1,0,2:T(8,128)(2,1)S(1)} %copy.114), channel_id=1, replica_groups=mesh['gx'=4,'gy'=2,'gz'=4] {'gy'}, dimensions={2} | all-to-all | bytes 1572864 | tf_op jit(solution)/shard_map/all_to_all | solution.py:169
  (139 shorter events, 74.6 us)
Async XLA Ops:
  4.8 5.2 %collective-permute-start.1 = (bf16[3,1,8,128]{3,2,1,0:T(8,128)(2,1)S(1)}, bf16[3,1,8,128]{3,2,1,0:T(8,128)(2,1)S(1)}, u32[]{:S(2)}, u32[]{:S(2)}) collective-permute-start(bf16[3,1,8,128]{3,2,1,0:T(8,128)(2,1)S(1)} %get-tuple-element.67), channel_id=1, source_target_pairs={{8,0},{16,8},{24,16},{9,1},{17,9},{25,17},{10,2},{18,10},{26,18},{... | collective-permute-start | bytes 18440 | tf_op jit(solution)/shard_map/ppermute | solution.py:20
  10.5 5.6 %collective-permute-start.2 = (bf16[3,66,1,128]{1,3,2,0:T(8,128)(2,1)S(1)}, bf16[3,66,1,128]{1,3,2,0:T(8,128)(2,1)S(1)}, u32[]{:S(2)}, u32[]{:S(2)}) collective-permute-start(bf16[3,66,1,128]{1,3,2,0:T(8,128)(2,1)S(1)} %get-tuple-element.55), channel_id=1, source_target_pairs={{0,4},{1,5},{2,6},{3,7},{8,12},{9,13},{10,14},{11,15},{16,20},{17,... | collective-permute-start | bytes 152072 | tf_op jit(solution)/shard_map/ppermute | solution.py:19
  14.0 6.5 %collective-permute-start.3 = (bf16[3,66,1,128]{1,3,2,0:T(8,128)(2,1)S(1)}, bf16[3,66,1,128]{1,3,2,0:T(8,128)(2,1)S(1)}, u32[]{:S(2)}, u32[]{:S(2)}) collective-permute-start(bf16[3,66,1,128]{1,3,2,0:T(8,128)(2,1)S(1)} %get-tuple-element.56), channel_id=1, source_target_pairs={{4,0},{5,1},{6,2},{7,3},{12,8},{13,9},{14,10},{15,11},{20,16},{21,... | collective-permute-start | bytes 152072 | tf_op jit(solution)/shard_map/ppermute | solution.py:20
  20.5 5.0 %collective-permute-start.4 = (bf16[3,66,10,1]{1,0,3,2:T(4,128)(2,1)S(1)}, bf16[3,66,10,1]{1,0,3,2:T(4,128)(2,1)S(1)}, u32[]{:S(2)}, u32[]{:S(2)}) collective-permute-start(bf16[3,66,10,1]{1,0,3,2:T(4,128)(2,1)S(1)} %copy.93), channel_id=1, source_target_pairs={{0,1},{1,2},{2,3},{4,5},{5,6},{6,7},{8,9},{9,10},{10,11},{12,13},{... | collective-permute-start | bytes 11888 | tf_op jit(solution)/shard_map/ppermute | solution.py:19
  24.0 5.6 %collective-permute-start.5 = (bf16[3,66,10,1]{1,0,3,2:T(4,128)(2,1)S(1)}, bf16[3,66,10,1]{1,0,3,2:T(4,128)(2,1)S(1)}, u32[]{:S(2)}, u32[]{:S(2)}) collective-permute-start(bf16[3,66,10,1]{1,0,3,2:T(4,128)(2,1)S(1)} %copy.94), channel_id=1, source_target_pairs={{1,0},{2,1},{3,2},{5,4},{6,5},{7,6},{9,8},{10,9},{11,10},{13,12},{... | collective-permute-start | bytes 11888 | tf_op jit(solution)/shard_map/ppermute | solution.py:20
  37.1 6.9 %collective-permute-start.8 = (f32[68,2,128]{0,2,1:T(8,128)S(1)}, f32[68,2,128]{0,2,1:T(8,128)S(1)}, u32[]{:S(2)}, u32[]{:S(2)}) collective-permute-start(f32[68,2,128]{0,2,1:T(8,128)S(1)} %get-tuple-element.40), channel_id=1, source_target_pairs={{4,0},{5,1},{6,2},{7,3},{12,8},{13,9},{14,10},{15,11},{20,16},{21,... | collective-permute-start | bytes 208904 | tf_op jit(solution)/shard_map/ppermute | solution.py:20
  38.4 7.1 %collective-permute-start.9 = (f32[68,2,128]{0,2,1:T(8,128)S(1)}, f32[68,2,128]{0,2,1:T(8,128)S(1)}, u32[]{:S(2)}, u32[]{:S(2)}) collective-permute-start(f32[68,2,128]{0,2,1:T(8,128)S(1)} %get-tuple-element.39), channel_id=1, source_target_pairs={{0,4},{1,5},{2,6},{3,7},{8,12},{9,13},{10,14},{11,15},{16,20},{17,... | collective-permute-start | bytes 208904 | tf_op jit(solution)/shard_map/ppermute | solution.py:19
  45.6 5.9 %collective-permute-start.10 = (f32[68,12,2]{0,2,1:T(2,128)S(1)}, f32[68,12,2]{0,2,1:T(2,128)S(1)}, u32[]{:S(2)}, u32[]{:S(2)}) collective-permute-start(f32[68,12,2]{0,2,1:T(2,128)S(1)} %get-tuple-element.33), channel_id=1, source_target_pairs={{1,0},{2,1},{3,2},{5,4},{6,5},{7,6},{9,8},{10,9},{11,10},{13,12},{... | collective-permute-start | bytes 19592 | tf_op jit(solution)/shard_map/ppermute | solution.py:20
  46.9 5.9 %collective-permute-start.11 = (f32[68,12,2]{0,2,1:T(2,128)S(1)}, f32[68,12,2]{0,2,1:T(2,128)S(1)}, u32[]{:S(2)}, u32[]{:S(2)}) collective-permute-start(f32[68,12,2]{0,2,1:T(2,128)S(1)} %get-tuple-element.34), channel_id=1, source_target_pairs={{0,1},{1,2},{2,3},{4,5},{5,6},{6,7},{8,9},{9,10},{10,11},{12,13},{... | collective-permute-start | bytes 19592 | tf_op jit(solution)/shard_map/ppermute | solution.py:19
  54.7 8.1 %collective-permute-start.12 = (f32[2,8,128]{0,2,1:T(8,128)S(1)}, f32[2,8,128]{0,2,1:T(8,128)S(1)}, u32[]{:S(2)}, u32[]{:S(2)}) collective-permute-start(f32[2,8,128]{0,2,1:T(8,128)S(1)} %get-tuple-element.63), channel_id=1, source_target_pairs={{8,0},{16,8},{24,16},{9,1},{17,9},{25,17},{10,2},{18,10},{26,18},{... | collective-permute-start | bytes 24584 | tf_op jit(solution)/shard_map/ppermute | solution.py:20
  56.0 8.3 %collective-permute-start.13 = (f32[2,8,128]{0,2,1:T(8,128)S(1)}, f32[2,8,128]{0,2,1:T(8,128)S(1)}, u32[]{:S(2)}, u32[]{:S(2)}) collective-permute-start(f32[2,8,128]{0,2,1:T(8,128)S(1)} %get-tuple-element.62), channel_id=1, source_target_pairs={{0,8},{8,16},{16,24},{1,9},{9,17},{17,25},{2,10},{10,18},{18,26},{... | collective-permute-start | bytes 24584 | tf_op jit(solution)/shard_map/ppermute | solution.py:19
  64.5 6.9 %collective-permute-start.14 = (f32[68,2,128]{0,2,1:T(8,128)S(1)}, f32[68,2,128]{0,2,1:T(8,128)S(1)}, u32[]{:S(2)}, u32[]{:S(2)}) collective-permute-start(f32[68,2,128]{0,2,1:T(8,128)S(1)} %get-tuple-element.38), channel_id=1, source_target_pairs={{4,0},{5,1},{6,2},{7,3},{12,8},{13,9},{14,10},{15,11},{20,16},{21,... | collective-permute-start | bytes 208904 | tf_op jit(solution)/shard_map/ppermute | solution.py:20
  65.8 7.1 %collective-permute-start.15 = (f32[68,2,128]{0,2,1:T(8,128)S(1)}, f32[68,2,128]{0,2,1:T(8,128)S(1)}, u32[]{:S(2)}, u32[]{:S(2)}) collective-permute-start(f32[68,2,128]{0,2,1:T(8,128)S(1)} %get-tuple-element.37), channel_id=1, source_target_pairs={{0,4},{1,5},{2,6},{3,7},{8,12},{9,13},{10,14},{11,15},{16,20},{17,... | collective-permute-start | bytes 208904 | tf_op jit(solution)/shard_map/ppermute | solution.py:19
  73.0 5.9 %collective-permute-start.16 = (f32[68,12,2]{0,2,1:T(2,128)S(1)}, f32[68,12,2]{0,2,1:T(2,128)S(1)}, u32[]{:S(2)}, u32[]{:S(2)}) collective-permute-start(f32[68,12,2]{0,2,1:T(2,128)S(1)} %get-tuple-element.31), channel_id=1, source_target_pairs={{1,0},{2,1},{3,2},{5,4},{6,5},{7,6},{9,8},{10,9},{11,10},{13,12},{... | collective-permute-start | bytes 19592 | tf_op jit(solution)/shard_map/ppermute | solution.py:20
  74.3 5.9 %collective-permute-start.17 = (f32[68,12,2]{0,2,1:T(2,128)S(1)}, f32[68,12,2]{0,2,1:T(2,128)S(1)}, u32[]{:S(2)}, u32[]{:S(2)}) collective-permute-start(f32[68,12,2]{0,2,1:T(2,128)S(1)} %get-tuple-element.32), channel_id=1, source_target_pairs={{0,1},{1,2},{2,3},{4,5},{5,6},{6,7},{8,9},{9,10},{10,11},{12,13},{... | collective-permute-start | bytes 19592 | tf_op jit(solution)/shard_map/ppermute | solution.py:19
  82.1 11.1 %collective-permute-start.18 = (f32[2,8,128]{0,2,1:T(8,128)S(1)}, f32[2,8,128]{0,2,1:T(8,128)S(1)}, u32[]{:S(2)}, u32[]{:S(2)}) collective-permute-start(f32[2,8,128]{0,2,1:T(8,128)S(1)} %get-tuple-element.60), channel_id=1, source_target_pairs={{0,8},{8,16},{16,24},{1,9},{9,17},{17,25},{2,10},{10,18},{18,26},{... | collective-permute-start | bytes 24584 | tf_op jit(solution)/shard_map/ppermute | solution.py:19
  91.8 7.7 %collective-permute-start.19 = (f32[2,8,128]{0,2,1:T(8,128)S(1)}, f32[2,8,128]{0,2,1:T(8,128)S(1)}, u32[]{:S(2)}, u32[]{:S(2)}) collective-permute-start(f32[2,8,128]{0,2,1:T(8,128)S(1)} %get-tuple-element.61), channel_id=1, source_target_pairs={{8,0},{16,8},{24,16},{9,1},{17,9},{25,17},{10,2},{18,10},{26,18},{... | collective-permute-start | bytes 24584 | tf_op jit(solution)/shard_map/ppermute | solution.py:20
  99.6 6.9 %collective-permute-start.20 = (f32[68,2,128]{0,2,1:T(8,128)S(1)}, f32[68,2,128]{0,2,1:T(8,128)S(1)}, u32[]{:S(2)}, u32[]{:S(2)}) collective-permute-start(f32[68,2,128]{0,2,1:T(8,128)S(1)} %get-tuple-element.35), channel_id=1, source_target_pairs={{0,4},{1,5},{2,6},{3,7},{8,12},{9,13},{10,14},{11,15},{16,20},{17,... | collective-permute-start | bytes 208904 | tf_op jit(solution)/shard_map/ppermute | solution.py:19
  104.0 6.9 %collective-permute-start.21 = (f32[68,2,128]{0,2,1:T(8,128)S(1)}, f32[68,2,128]{0,2,1:T(8,128)S(1)}, u32[]{:S(2)}, u32[]{:S(2)}) collective-permute-start(f32[68,2,128]{0,2,1:T(8,128)S(1)} %get-tuple-element.36), channel_id=1, source_target_pairs={{4,0},{5,1},{6,2},{7,3},{12,8},{13,9},{14,10},{15,11},{20,16},{21,... | collective-permute-start | bytes 208904 | tf_op jit(solution)/shard_map/ppermute | solution.py:20
  111.0 5.7 %collective-permute-start.22 = (f32[68,12,2]{0,2,1:T(2,128)S(1)}, f32[68,12,2]{0,2,1:T(2,128)S(1)}, u32[]{:S(2)}, u32[]{:S(2)}) collective-permute-start(f32[68,12,2]{0,2,1:T(2,128)S(1)} %get-tuple-element.29), channel_id=1, source_target_pairs={{0,1},{1,2},{2,3},{4,5},{5,6},{6,7},{8,9},{9,10},{10,11},{12,13},{... | collective-permute-start | bytes 19592 | tf_op jit(solution)/shard_map/ppermute | solution.py:19
  115.2 5.6 %collective-permute-start.23 = (f32[68,12,2]{0,2,1:T(2,128)S(1)}, f32[68,12,2]{0,2,1:T(2,128)S(1)}, u32[]{:S(2)}, u32[]{:S(2)}) collective-permute-start(f32[68,12,2]{0,2,1:T(2,128)S(1)} %get-tuple-element.30), channel_id=1, source_target_pairs={{1,0},{2,1},{3,2},{5,4},{6,5},{7,6},{9,8},{10,9},{11,10},{13,12},{... | collective-permute-start | bytes 19592 | tf_op jit(solution)/shard_map/ppermute | solution.py:20
  126.6 9.3 %all-to-all-start = ((bf16[3,64,8,128]{3,2,0,1:T(8,128)(2,1)}), bf16[3,64,8,128]{3,2,0,1:T(8,128)(2,1)S(1)}, u32[]{:S(2)}, u32[]{:S(2)}) async-start(bf16[3,64,8,128]{3,2,0,1:T(8,128)(2,1)} %copy.99), calls=%async_computation | async-start | bytes 786432 | tf_op jit(solution)/shard_map/all_to_all | solution.py:161
  138.1 8.8 %collective-permute-start.25 = (f32[3,1,16,128]{3,2,1,0:T(8,128)S(1)}, f32[3,1,16,128]{3,2,1,0:T(8,128)S(1)}, u32[]{:S(2)}, u32[]{:S(2)}) collective-permute-start(f32[3,1,16,128]{3,2,1,0:T(8,128)S(1)} %get-tuple-element.54), channel_id=1, source_target_pairs={{4,0},{8,4},{12,8},{16,12},{20,16},{24,20},{28,24},{5,1},{9,5},{13... | collective-permute-start | bytes 73736 | tf_op jit(solution)/shard_map/ppermute | solution.py:20
  147.7 5.4 %collective-permute-start.26 = (f32[3,34,16,1]{1,2,3,0:T(8,128)S(1)}, f32[3,34,16,1]{1,2,3,0:T(8,128)S(1)}, u32[]{:S(2)}, u32[]{:S(2)}) collective-permute-start(f32[3,34,16,1]{1,2,3,0:T(8,128)S(1)} %copy.102), channel_id=1, source_target_pairs={{0,1},{1,2},{2,3},{4,5},{5,6},{6,7},{8,9},{9,10},{10,11},{12,13},{... | collective-permute-start | bytes 19592 | tf_op jit(solution)/shard_map/ppermute | solution.py:19
  151.8 5.7 %collective-permute-start.27 = (f32[3,34,16,1]{1,2,3,0:T(8,128)S(1)}, f32[3,34,16,1]{1,2,3,0:T(8,128)S(1)}, u32[]{:S(2)}, u32[]{:S(2)}) collective-permute-start(f32[3,34,16,1]{1,2,3,0:T(8,128)S(1)} %copy.103), channel_id=1, source_target_pairs={{1,0},{2,1},{3,2},{5,4},{6,5},{7,6},{9,8},{10,9},{11,10},{13,12},{... | collective-permute-start | bytes 19592 | tf_op jit(solution)/shard_map/ppermute | solution.py:20
  162.5 4.9 %collective-permute-start.28 = (f32[3,1,16,128]{3,2,1,0:T(8,128)S(1)}, f32[3,1,16,128]{3,2,1,0:T(8,128)S(1)}, u32[]{:S(2)}, u32[]{:S(2)}) collective-permute-start(f32[3,1,16,128]{3,2,1,0:T(8,128)S(1)} %get-tuple-element.51), channel_id=1, source_target_pairs={{0,4},{4,8},{8,12},{12,16},{16,20},{20,24},{24,28},{1,5},{5,9},{9,... | collective-permute-start | bytes 73736 | tf_op jit(solution)/shard_map/ppermute | solution.py:19
  165.8 5.7 %collective-permute-start.29 = (f32[3,1,16,128]{3,2,1,0:T(8,128)S(1)}, f32[3,1,16,128]{3,2,1,0:T(8,128)S(1)}, u32[]{:S(2)}, u32[]{:S(2)}) collective-permute-start(f32[3,1,16,128]{3,2,1,0:T(8,128)S(1)} %get-tuple-element.52), channel_id=1, source_target_pairs={{4,0},{8,4},{12,8},{16,12},{20,16},{24,20},{28,24},{5,1},{9,5},{13... | collective-permute-start | bytes 73736 | tf_op jit(solution)/shard_map/ppermute | solution.py:20
  172.3 5.2 %collective-permute-start.30 = (f32[3,34,16,1]{1,2,3,0:T(8,128)S(1)}, f32[3,34,16,1]{1,2,3,0:T(8,128)S(1)}, u32[]{:S(2)}, u32[]{:S(2)}) collective-permute-start(f32[3,34,16,1]{1,2,3,0:T(8,128)S(1)} %copy.106), channel_id=1, source_target_pairs={{0,1},{1,2},{2,3},{4,5},{5,6},{6,7},{8,9},{9,10},{10,11},{12,13},{... | collective-permute-start | bytes 19592 | tf_op jit(solution)/shard_map/ppermute | solution.py:19
  176.3 5.7 %collective-permute-start.31 = (f32[3,34,16,1]{1,2,3,0:T(8,128)S(1)}, f32[3,34,16,1]{1,2,3,0:T(8,128)S(1)}, u32[]{:S(2)}, u32[]{:S(2)}) collective-permute-start(f32[3,34,16,1]{1,2,3,0:T(8,128)S(1)} %copy.107), channel_id=1, source_target_pairs={{1,0},{2,1},{3,2},{5,4},{6,5},{7,6},{9,8},{10,9},{11,10},{13,12},{... | collective-permute-start | bytes 19592 | tf_op jit(solution)/shard_map/ppermute | solution.py:20
  187.1 5.6 %collective-permute-start.32 = (f32[3,1,16,128]{3,2,1,0:T(8,128)S(1)}, f32[3,1,16,128]{3,2,1,0:T(8,128)S(1)}, u32[]{:S(2)}, u32[]{:S(2)}) collective-permute-start(f32[3,1,16,128]{3,2,1,0:T(8,128)S(1)} %get-tuple-element.49), channel_id=1, source_target_pairs={{0,4},{4,8},{8,12},{12,16},{16,20},{20,24},{24,28},{1,5},{5,9},{9,... | collective-permute-start | bytes 73736 | tf_op jit(solution)/shard_map/ppermute | solution.py:19
  191.2 5.9 %collective-permute-start.33 = (f32[3,1,16,128]{3,2,1,0:T(8,128)S(1)}, f32[3,1,16,128]{3,2,1,0:T(8,128)S(1)}, u32[]{:S(2)}, u32[]{:S(2)}) collective-permute-start(f32[3,1,16,128]{3,2,1,0:T(8,128)S(1)} %get-tuple-element.50), channel_id=1, source_target_pairs={{4,0},{8,4},{12,8},{16,12},{20,16},{24,20},{28,24},{5,1},{9,5},{13... | collective-permute-start | bytes 73736 | tf_op jit(solution)/shard_map/ppermute | solution.py:20
  200.5 5.7 %collective-permute-start.35 = (f32[3,34,16,1]{1,2,3,0:T(8,128)S(1)}, f32[3,34,16,1]{1,2,3,0:T(8,128)S(1)}, u32[]{:S(2)}, u32[]{:S(2)}) collective-permute-start(f32[3,34,16,1]{1,2,3,0:T(8,128)S(1)} %copy.111), channel_id=1, source_target_pairs={{1,0},{2,1},{3,2},{5,4},{6,5},{7,6},{9,8},{10,9},{11,10},{13,12},{... | collective-permute-start | bytes 19592 | tf_op jit(solution)/shard_map/ppermute | solution.py:20
  (13 other events, 63.5 us)
where the time goes:
time: 226 us; the launch traced here: 225 us
  starting transfers between devices  101 us (45%)
  waiting for transfers between devices  73.7 us (33%)
  other arithmetic  22.4 us (10%)
  local copies, waits for them, and re-layouts  13.2 us (6%)
  blocking collectives  13.2 us (6%)
    ppermute x18, starting transfers between devices, padded_2(): before = lax.ppermute(last, axis, up)  74.2 us
    ppermute x18, waiting for transfers between devices, padded_2(): after = lax.ppermute(leading, axis, down)  56.5 us
    ppermute x18, starting transfers between devices, padded_2(): after = lax.ppermute(leading, axis, down)  23.6 us
    all_to_all x1, blocking collectives, per_device(): return lax.all_to_all(strain, 'gy', split_axis=2, concat_axis=1, tiled=True)  13.2 us
    ppermute x18, waiting for transfers between devices, padded_2(): before = lax.ppermute(last, axis, up)  11.4 us
    all_to_all x1, waiting for transfers between devices, per_device(): lax.all_to_all(force, 'gy', split_axis=1, concat_axis=2, tiled=True)  5.82 us
    another operation x6, other arithmetic, navier(): return jnp.stack(result)  5.01 us
    concatenate x10, other arithmetic, padded_2(): value = jnp.concatenate([before, value, after], axis=dim)  4.53 us
  transfers between devices with their start and end apart: 37, of which 26 were waited for; matrix products, arithmetic and copies ran while one was open for 1% of the time, Pallas kernels for 0%

commit v1 on v0

--- a/solution.py
+++ b/solution.py
@@ -166,7 +166,10 @@
 
     displacement = elastic_solve(load, stiffness, pad_slab)
     strain = strain_from(pad_slab(displacement)).astype(jnp.bfloat16)
-    return lax.all_to_all(strain, "gy", split_axis=2, concat_axis=1, tiled=True)
+    return jnp.concatenate(
+        lax.all_to_all(jnp.stack(jnp.split(strain, lax.axis_size("gy"), axis=2)), "gy", 0, 0),
+        axis=1,
+    )
 
 
 def solution(mesh):

time: 226 us -> 237 us (1.049)
  local copies, waits for them, and re-layouts: 13.2 us -> 38.7 us
  starting transfers between devices: 101 us -> 89.4 us
  waiting for transfers between devices: 73.7 us -> 62.6 us
  other arithmetic: 22.4 us -> 30.5 us
    ppermute x18, starting transfers between devices: 74.2 us -> 62.4 us  [padded_2(): before = lax.ppermute(last, axis, up)]
    ppermute x18, waiting for transfers between devices: 56.5 us -> 48.9 us  [padded_2(): after = lax.ppermute(leading, axis, down)]
    slice x4 -> x7, local copies, waits for them, and re-layouts: 1.36 us -> 7.52 us  [padded_2(): leading = lax.slice_in_dim(value, 0, width, axis=dim)]
    ppermute x4 -> x8, local copies, waits for them, and re-layouts: 1.51 us -> 7.23 us  [padded_2(): after = lax.ppermute(leading, axis, down)]
    ppermute x4 -> x8, local copies, waits for them, and re-layouts: 1.51 us -> 7.17 us  [padded_2(): before = lax.ppermute(last, axis, up)]
    ppermute x18, waiting for transfers between devices: 11.4 us -> 6.56 us  [padded_2(): before = lax.ppermute(last, axis, up)]
    slice x15 -> x17, local copies, waits for them, and re-layouts: 2.88 us -> 7.61 us  [padded_2(): last = lax.slice_in_dim(value, length - width, length, axis=dim)]
    unnamed x18 -> x48, local copies, waits for them, and re-layouts: 2 us -> 6.43 us
  transfers between devices with their start and end apart: 37 -> 37, of which waited for: 26 -> 24; matrix products, arithmetic and copies ran while one was open for 1% -> 6% of each run, Pallas kernels for 0% -> 0%
where the time goes in v1:
time: 237 us; the launch traced here: 235 us
  starting transfers between devices  89.4 us (38%)
  waiting for transfers between devices  62.6 us (26%)
  local copies, waits for them, and re-layouts  38.7 us (16%)
  other arithmetic  30.5 us (13%)
  blocking collectives  13.2 us (6%)
    ppermute x18, starting transfers between devices, padded_2(): before = lax.ppermute(last, axis, up)  62.4 us
    ppermute x18, waiting for transfers between devices, padded_2(): after = lax.ppermute(leading, axis, down)  48.9 us
    ppermute x18, starting transfers between devices, padded_2(): after = lax.ppermute(leading, axis, down)  23.6 us
    all_to_all x1, blocking collectives, per_device(): lax.all_to_all(jnp.stack(jnp.split(strain, lax.axis_size('gy'), axis=2)),...  13.2 us
    slice x17, local copies, waits for them, and re-layouts, padded_2(): last = lax.slice_in_dim(value, length - width, length, axis=dim)  7.61 us
    slice x7, local copies, waits for them, and re-layouts, padded_2(): leading = lax.slice_in_dim(value, 0, width, axis=dim)  7.52 us
    ppermute x8, local copies, waits for them, and re-layouts, padded_2(): after = lax.ppermute(leading, axis, down)  7.23 us
    ppermute x8, local copies, waits for them, and re-layouts, padded_2(): before = lax.ppermute(last, axis, up)  7.17 us
  transfers between devices with their start and end apart: 37, of which 24 were waited for; matrix products, arithmetic and copies ran while one was open for 6% of the time, Pallas kernels for 0%

profile of v1, /device:TPU:0, one launch (start us, length us, event | category | flops | bytes accessed | tf_op | source)
XLA Modules:
  0.0 235.3 jit_solution(17034764095796212313)
XLA Ops:
  5.7 3.9 %collective-permute-done.1 = bf16[3,1,8,128]{3,2,1,0:T(8,128)(2,1)S(1)} collective-permute-done((bf16[3,1,8,128]{3,2,1,0:T(8,128)(2,1)S(1)}, bf16[3,1,8,128]{3,2,1,0:T(8,128)(2,1)S(1)}, u32[]{:S(2)}, u32[]{:S(2)}) %collective-permute-start.1) | collective-permute-done | bytes 6176 | tf_op jit(solution)/shard_map/ppermute | solution.py:20
  9.7 3.4 %collective-permute-start.2 = (bf16[3,66,1,128]{3,1,2,0:T(8,128)(2,1)S(1)}, bf16[3,66,1,128]{3,1,2,0:T(8,128)(2,1)S(1)}, u32[]{:S(2)}, u32[]{:S(2)}) collective-permute-start(bf16[3,66,1,128]{3,1,2,0:T(8,128)(2,1)S(1)} %copy.120), channel_id=1, source_target_pairs={{0,4},{1,5},{2,6},{3,7},{8,12},{9,13},{10,14},{11,15},{16,20},{17,... | collective-permute-start | bytes 152072 | tf_op jit(solution)/shard_map/ppermute | solution.py:19
  15.0 4.2 %collective-permute-done.3 = bf16[3,66,1,128]{3,1,2,0:T(8,128)(2,1)S(1)} collective-permute-done((bf16[3,66,1,128]{3,1,2,0:T(8,128)(2,1)S(1)}, bf16[3,66,1,128]{3,1,2,0:T(8,128)(2,1)S(1)}, u32[]{:S(2)}, u32[]{:S(2)}) %collective-permute-start.3) | collective-permute-done | bytes 50720 | tf_op jit(solution)/shard_map/ppermute | solution.py:20
  21.0 3.5 %collective-permute-start.4 = (bf16[3,66,10,1]{1,2,3,0:T(8,128)(2,1)S(1)}, bf16[3,66,10,1]{1,2,3,0:T(8,128)(2,1)S(1)}, u32[]{:S(2)}, u32[]{:S(2)}) collective-permute-start(bf16[3,66,10,1]{1,2,3,0:T(8,128)(2,1)S(1)} %copy.124), channel_id=1, source_target_pairs={{0,1},{1,2},{2,3},{4,5},{5,6},{6,7},{8,9},{9,10},{10,11},{12,13},{... | collective-permute-start | bytes 11888 | tf_op jit(solution)/shard_map/ppermute | solution.py:19
  28.1 2.7 %collective-permute-done.5 = bf16[3,66,10,1]{1,2,3,0:T(8,128)(2,1)S(1)} collective-permute-done((bf16[3,66,10,1]{1,2,3,0:T(8,128)(2,1)S(1)}, bf16[3,66,10,1]{1,2,3,0:T(8,128)(2,1)S(1)}, u32[]{:S(2)}, u32[]{:S(2)}) %collective-permute-start.5) | collective-permute-done | bytes 3992 | tf_op jit(solution)/shard_map/ppermute | solution.py:20
  32.4 3.2 %maximum_convert_fusion = f32[3,66,10,130]{3,2,1,0:T(8,128)S(1)} fusion(bf16[3,66,10,1]{3,2,1,0:T(8,128)(2,1)} %copy.127, bf16[3,66,1,128]{3,2,1,0:T(2,128)(2,1)S(1)} %copy.123, bf16[3,1,8,128]{3,2,1,0:T(8,128)(2,1)S(1)} %collective-permute-done.1, bf16[3,64,8,128]{3,2,1,0:T(8,128)(2,1)} %copy-done, bf16[3,1,8,128]{3,2,1,0:T(8,128)(2,1)S(1)} %collective-permute-done, ...), kind=kLoop, calls=%fused_computation.15 | loop fusion | flops 3603600 | bytes 1544400 | tf_op jit(solution)/shard_map/convert_element_type | solution.py:147
  39.0 3.0 %collective-permute-start.7 = (f32[2,8,128]{2,1,0:T(8,128)S(1)}, f32[2,8,128]{2,1,0:T(8,128)S(1)}, u32[]{:S(2)}, u32[]{:S(2)}) collective-permute-start(f32[2,8,128]{2,1,0:T(8,128)S(1)} %get-tuple-element.68), channel_id=1, source_target_pairs={{0,8},{8,16},{16,24},{1,9},{9,17},{17,25},{2,10},{10,18},{18,26},{... | collective-permute-start | bytes 24584 | tf_op jit(solution)/shard_map/ppermute | solution.py:19
  44.2 4.5 %collective-permute-start.9 = (f32[68,2,128]{2,1,0:T(2,128)S(1)}, f32[68,2,128]{2,1,0:T(2,128)S(1)}, u32[]{:S(2)}, u32[]{:S(2)}) collective-permute-start(f32[68,2,128]{2,1,0:T(2,128)S(1)} %get-tuple-element.62), channel_id=1, source_target_pairs={{0,4},{1,5},{2,6},{3,7},{8,12},{9,13},{10,14},{11,15},{16,20},{17,... | collective-permute-start | bytes 208904 | tf_op jit(solution)/shard_map/ppermute | solution.py:19
  57.1 5.1 %collective-permute-start.11 = (f32[68,12,2]{0,2,1:T(2,128)}, f32[68,12,2]{0,2,1:T(2,128)}, u32[]{:S(2)}, u32[]{:S(2)}) collective-permute-start(f32[68,12,2]{0,2,1:T(2,128)} %copy.130), channel_id=1, source_target_pairs={{0,1},{1,2},{2,3},{4,5},{5,6},{6,7},{8,9},{9,10},{10,11},{12,13},{... | collective-permute-start | bytes 19592 | tf_op jit(solution)/shard_map/ppermute | solution.py:19
  68.5 3.0 %collective-permute-start.13 = (f32[2,8,128]{2,1,0:T(8,128)S(1)}, f32[2,8,128]{2,1,0:T(8,128)S(1)}, u32[]{:S(2)}, u32[]{:S(2)}) collective-permute-start(f32[2,8,128]{2,1,0:T(8,128)S(1)} %get-tuple-element.66), channel_id=1, source_target_pairs={{0,8},{8,16},{16,24},{1,9},{9,17},{17,25},{2,10},{10,18},{18,26},{... | collective-permute-start | bytes 24584 | tf_op jit(solution)/shard_map/ppermute | solution.py:19
  73.7 4.5 %collective-permute-start.15 = (f32[68,2,128]{2,1,0:T(2,128)S(1)}, f32[68,2,128]{2,1,0:T(2,128)S(1)}, u32[]{:S(2)}, u32[]{:S(2)}) collective-permute-start(f32[68,2,128]{2,1,0:T(2,128)S(1)} %get-tuple-element.60), channel_id=1, source_target_pairs={{0,4},{1,5},{2,6},{3,7},{8,12},{9,13},{10,14},{11,15},{16,20},{17,... | collective-permute-start | bytes 208904 | tf_op jit(solution)/shard_map/ppermute | solution.py:19
  85.9 4.8 %collective-permute-start.17 = (f32[68,12,2]{0,2,1:T(2,128)S(1)}, f32[68,12,2]{0,2,1:T(2,128)S(1)}, u32[]{:S(2)}, u32[]{:S(2)}) collective-permute-start(f32[68,12,2]{0,2,1:T(2,128)S(1)} %copy.134), channel_id=1, source_target_pairs={{0,1},{1,2},{2,3},{4,5},{5,6},{6,7},{8,9},{9,10},{10,11},{12,13},{... | collective-permute-start | bytes 19592 | tf_op jit(solution)/shard_map/ppermute | solution.py:19
  93.2 2.7 %fusion.103 = f32[64,8,128]{2,1,0:T(8,128)S(1)} fusion(f32[64,8,128]{2,1,0:T(8,128)} %copy-done.3, f32[64,8,128]{2,1,0:T(8,128)} %get-tuple-element.11, f32[68,12,2]{2,1,0:T(8,128)} %copy.135, f32[68,2,128]{2,1,0:T(2,128)} %copy-done.18, f32[68,2,128]{2,1,0:T(2,128)} %copy-done.20, f32[2,8,128]{2,1,0:T(8,128)S(1)} %collective-permute-done.12, ...), kind=kLoop, calls=%fused_computation.240 | loop fusion | flops 2359296 | bytes 1479424 | tf_op jit(solution)/shard_map/add | solution.py:155
  95.9 3.8 %collective-permute-start.18 = (f32[2,8,128]{2,1,0:T(8,128)S(1)}, f32[2,8,128]{2,1,0:T(8,128)S(1)}, u32[]{:S(2)}, u32[]{:S(2)}) collective-permute-start(f32[2,8,128]{2,1,0:T(8,128)S(1)} %get-tuple-element.64), channel_id=1, source_target_pairs={{0,8},{8,16},{16,24},{1,9},{9,17},{17,25},{2,10},{10,18},{18,26},{... | collective-permute-start | bytes 24584 | tf_op jit(solution)/shard_map/ppermute | solution.py:19
  101.1 5.2 %collective-permute-done.19 = f32[2,8,128]{2,1,0:T(8,128)S(1)} collective-permute-done((f32[2,8,128]{2,1,0:T(8,128)S(1)}, f32[2,8,128]{2,1,0:T(8,128)S(1)}, u32[]{:S(2)}, u32[]{:S(2)}) %collective-permute-start.19) | collective-permute-done | bytes 8224 | tf_op jit(solution)/shard_map/ppermute | solution.py:20
  106.3 4.3 %collective-permute-start.20 = (f32[68,2,128]{2,1,0:T(2,128)S(1)}, f32[68,2,128]{2,1,0:T(2,128)S(1)}, u32[]{:S(2)}, u32[]{:S(2)}) collective-permute-start(f32[68,2,128]{2,1,0:T(2,128)S(1)} %get-tuple-element.58), channel_id=1, source_target_pairs={{0,4},{1,5},{2,6},{3,7},{8,12},{9,13},{10,14},{11,15},{16,20},{17,... | collective-permute-start | bytes 208904 | tf_op jit(solution)/shard_map/ppermute | solution.py:19
  112.5 4.3 %collective-permute-done.21 = f32[68,2,128]{2,1,0:T(2,128)S(1)} collective-permute-done((f32[68,2,128]{2,1,0:T(2,128)S(1)}, f32[68,2,128]{2,1,0:T(2,128)S(1)}, u32[]{:S(2)}, u32[]{:S(2)}) %collective-permute-start.21) | collective-permute-done | bytes 69664 | tf_op jit(solution)/shard_map/ppermute | solution.py:20
  120.0 4.2 %collective-permute-start.22 = (f32[68,12,2]{0,2,1:T(2,128)S(1)}, f32[68,12,2]{0,2,1:T(2,128)S(1)}, u32[]{:S(2)}, u32[]{:S(2)}) collective-permute-start(f32[68,12,2]{0,2,1:T(2,128)S(1)} %copy.136), channel_id=1, source_target_pairs={{0,1},{1,2},{2,3},{4,5},{5,6},{6,7},{8,9},{9,10},{10,11},{12,13},{... | collective-permute-start | bytes 19592 | tf_op jit(solution)/shard_map/ppermute | solution.py:19
  128.6 3.4 %collective-permute-done.23 = f32[68,12,2]{0,2,1:T(2,128)} collective-permute-done((f32[68,12,2]{0,2,1:T(2,128)}, f32[68,12,2]{0,2,1:T(2,128)}, u32[]{:S(2)}, u32[]{:S(2)}) %collective-permute-start.23) | collective-permute-done | bytes 6560 | tf_op jit(solution)/shard_map/ppermute | solution.py:20
  136.1 3.0 %subtract_multiply_fusion.2 = (f32[66,10,130]{2,1,0:T(8,128)S(1)}, f32[66,10,130]{2,1,0:T(8,128)S(1)}, f32[66,10,130]{2,1,0:T(8,128)S(1)}, f32[66,10,130]{2,1,0:T(8,128)S(1)}, f32[66,10,130]{2,1,0:T(8,128)S(1)}) fusion(f32[3,66,10,130]{3,2,1,0:T(8,128)S(1)} %maximum_convert_fusion, f32[68,12,132]{2,1,0:T(8,128)S(1)} %pad_maximum_fusion, ...), kind=kLoop, calls=%fused_computation.44 | loop fusion | flops 2488200 | bytes 4549248 | tf_op jit(solution)/shard_map/mul | solution.py:72
  142.0 3.5 %all-to-all-start = ((bf16[3,64,8,128]{3,2,0,1:T(8,128)(2,1)}), bf16[3,64,8,128]{3,2,0,1:T(8,128)(2,1)S(1)}, u32[]{:S(2)}, u32[]{:S(2)}) async-start(bf16[3,64,8,128]{3,2,0,1:T(8,128)(2,1)} %copy.142), calls=%async_computation | async-start | bytes 786432 | tf_op jit(solution)/shard_map/all_to_all | solution.py:161
  145.5 7.1 %all-to-all-done = bf16[3,64,8,128]{3,2,0,1:T(8,128)(2,1)S(1)} async-done(((bf16[3,64,8,128]{3,2,0,1:T(8,128)(2,1)}), bf16[3,64,8,128]{3,2,0,1:T(8,128)(2,1)S(1)}, u32[]{:S(2)}, u32[]{:S(2)}) %all-to-all-start) | async-done | bytes 393248 | tf_op jit(solution)/shard_map/all_to_all | solution.py:161
  156.4 4.2 %collective-permute-done.25 = f32[3,1,16,128]{3,2,1,0:T(8,128)S(1)} collective-permute-done((f32[3,1,16,128]{3,2,1,0:T(8,128)S(1)}, f32[3,1,16,128]{3,2,1,0:T(8,128)S(1)}, u32[]{:S(2)}, u32[]{:S(2)}) %collective-permute-start.25) | collective-permute-done | bytes 24608 | tf_op jit(solution)/shard_map/ppermute | solution.py:20
  161.5 3.2 %collective-permute-start.26 = (f32[3,34,16,1]{1,2,3,0:T(8,128)S(1)}, f32[3,34,16,1]{1,2,3,0:T(8,128)S(1)}, u32[]{:S(2)}, u32[]{:S(2)}) collective-permute-start(f32[3,34,16,1]{1,2,3,0:T(8,128)S(1)} %copy.157), channel_id=1, source_target_pairs={{0,1},{1,2},{2,3},{4,5},{5,6},{6,7},{8,9},{9,10},{10,11},{12,13},{... | collective-permute-start | bytes 19592 | tf_op jit(solution)/shard_map/ppermute | solution.py:19
  167.0 3.9 %collective-permute-done.27 = f32[3,34,16,1]{1,2,3,0:T(8,128)S(1)} collective-permute-done((f32[3,34,16,1]{1,2,3,0:T(8,128)S(1)}, f32[3,34,16,1]{1,2,3,0:T(8,128)S(1)}, u32[]{:S(2)}, u32[]{:S(2)}) %collective-permute-start.27) | collective-permute-done | bytes 6560 | tf_op jit(solution)/shard_map/ppermute | solution.py:20
  179.4 4.2 %collective-permute-done.29 = f32[3,1,16,128]{3,2,1,0:T(8,128)S(1)} collective-permute-done((f32[3,1,16,128]{3,2,1,0:T(8,128)S(1)}, f32[3,1,16,128]{3,2,1,0:T(8,128)S(1)}, u32[]{:S(2)}, u32[]{:S(2)}) %collective-permute-start.29) | collective-permute-done | bytes 24608 | tf_op jit(solution)/shard_map/ppermute | solution.py:20
  184.4 3.5 %collective-permute-start.30 = (f32[3,34,16,1]{1,2,3,0:T(8,128)S(1)}, f32[3,34,16,1]{1,2,3,0:T(8,128)S(1)}, u32[]{:S(2)}, u32[]{:S(2)}) collective-permute-start(f32[3,34,16,1]{1,2,3,0:T(8,128)S(1)} %copy.159), channel_id=1, source_target_pairs={{0,1},{1,2},{2,3},{4,5},{5,6},{6,7},{8,9},{9,10},{10,11},{12,13},{... | collective-permute-start | bytes 19592 | tf_op jit(solution)/shard_map/ppermute | solution.py:19
  190.1 3.9 %collective-permute-done.31 = f32[3,34,16,1]{1,2,3,0:T(8,128)S(1)} collective-permute-done((f32[3,34,16,1]{1,2,3,0:T(8,128)S(1)}, f32[3,34,16,1]{1,2,3,0:T(8,128)S(1)}, u32[]{:S(2)}, u32[]{:S(2)}) %collective-permute-start.31) | collective-permute-done | bytes 6560 | tf_op jit(solution)/shard_map/ppermute | solution.py:20
  199.1 3.1 %collective-permute-start.32 = (f32[3,1,16,128]{3,2,1,0:T(8,128)S(1)}, f32[3,1,16,128]{3,2,1,0:T(8,128)S(1)}, u32[]{:S(2)}, u32[]{:S(2)}) collective-permute-start(f32[3,1,16,128]{3,2,1,0:T(8,128)S(1)} %get-tuple-element.42), channel_id=1, source_target_pairs={{0,4},{4,8},{8,12},{12,16},{16,20},{20,24},{24,28},{1,5},{5,9},{9,... | collective-permute-start | bytes 73736 | tf_op jit(solution)/shard_map/ppermute | solution.py:19
  203.7 4.4 %collective-permute-done.33 = f32[3,1,16,128]{3,2,1,0:T(8,128)S(1)} collective-permute-done((f32[3,1,16,128]{3,2,1,0:T(8,128)S(1)}, f32[3,1,16,128]{3,2,1,0:T(8,128)S(1)}, u32[]{:S(2)}, u32[]{:S(2)}) %collective-permute-start.33) | collective-permute-done | bytes 24608 | tf_op jit(solution)/shard_map/ppermute | solution.py:20
  213.4 3.9 %collective-permute-done.35 = f32[3,34,16,1]{1,2,3,0:T(8,128)S(1)} collective-permute-done((f32[3,34,16,1]{1,2,3,0:T(8,128)S(1)}, f32[3,34,16,1]{1,2,3,0:T(8,128)S(1)}, u32[]{:S(2)}, u32[]{:S(2)}) %collective-permute-start.35) | collective-permute-done | bytes 6560 | tf_op jit(solution)/shard_map/ppermute | solution.py:20
  221.2 13.2 %all_to_all.14 = bf16[2,6,32,8,128]{4,3,2,1,0:T(8,128)(2,1)S(1)} all-to-all(bf16[2,6,32,8,128]{4,3,2,1,0:T(8,128)(2,1)S(1)} %pad_maximum_fusion.15), channel_id=1, replica_groups=mesh['gx'=4,'gy'=2,'gz'=4] {'gy'}, dimensions={0} | all-to-all | bytes 1572864 | tf_op jit(solution)/shard_map/all_to_all | solution.py:170
  (180 shorter events, 99.6 us)
Async XLA Ops:
  4.4 5.2 %collective-permute-start.1 = (bf16[3,1,8,128]{3,2,1,0:T(8,128)(2,1)S(1)}, bf16[3,1,8,128]{3,2,1,0:T(8,128)(2,1)S(1)}, u32[]{:S(2)}, u32[]{:S(2)}) collective-permute-start(bf16[3,1,8,128]{3,2,1,0:T(8,128)(2,1)S(1)} %get-tuple-element.57), channel_id=1, source_target_pairs={{8,0},{16,8},{24,16},{9,1},{17,9},{25,17},{10,2},{18,10},{26,18},{... | collective-permute-start | bytes 18440 | tf_op jit(solution)/shard_map/ppermute | solution.py:20
  9.7 5.2 %collective-permute-start.2 = (bf16[3,66,1,128]{3,1,2,0:T(8,128)(2,1)S(1)}, bf16[3,66,1,128]{3,1,2,0:T(8,128)(2,1)S(1)}, u32[]{:S(2)}, u32[]{:S(2)}) collective-permute-start(bf16[3,66,1,128]{3,1,2,0:T(8,128)(2,1)S(1)} %copy.120), channel_id=1, source_target_pairs={{0,4},{1,5},{2,6},{3,7},{8,12},{9,13},{10,14},{11,15},{16,20},{17,... | collective-permute-start | bytes 152072 | tf_op jit(solution)/shard_map/ppermute | solution.py:19
  13.2 6.0 %collective-permute-start.3 = (bf16[3,66,1,128]{3,1,2,0:T(8,128)(2,1)S(1)}, bf16[3,66,1,128]{3,1,2,0:T(8,128)(2,1)S(1)}, u32[]{:S(2)}, u32[]{:S(2)}) collective-permute-start(bf16[3,66,1,128]{3,1,2,0:T(8,128)(2,1)S(1)} %copy.121), channel_id=1, source_target_pairs={{4,0},{5,1},{6,2},{7,3},{12,8},{13,9},{14,10},{15,11},{20,16},{21,... | collective-permute-start | bytes 152072 | tf_op jit(solution)/shard_map/ppermute | solution.py:20
  21.0 5.5 %collective-permute-start.4 = (bf16[3,66,10,1]{1,2,3,0:T(8,128)(2,1)S(1)}, bf16[3,66,10,1]{1,2,3,0:T(8,128)(2,1)S(1)}, u32[]{:S(2)}, u32[]{:S(2)}) collective-permute-start(bf16[3,66,10,1]{1,2,3,0:T(8,128)(2,1)S(1)} %copy.124), channel_id=1, source_target_pairs={{0,1},{1,2},{2,3},{4,5},{5,6},{6,7},{8,9},{9,10},{10,11},{12,13},{... | collective-permute-start | bytes 11888 | tf_op jit(solution)/shard_map/ppermute | solution.py:19
  25.2 5.6 %collective-permute-start.5 = (bf16[3,66,10,1]{1,2,3,0:T(8,128)(2,1)S(1)}, bf16[3,66,10,1]{1,2,3,0:T(8,128)(2,1)S(1)}, u32[]{:S(2)}, u32[]{:S(2)}) collective-permute-start(bf16[3,66,10,1]{1,2,3,0:T(8,128)(2,1)S(1)} %copy.125), channel_id=1, source_target_pairs={{1,0},{2,1},{3,2},{5,4},{6,5},{7,6},{9,8},{10,9},{11,10},{13,12},{... | collective-permute-start | bytes 11888 | tf_op jit(solution)/shard_map/ppermute | solution.py:20
  37.7 4.3 %collective-permute-start.6 = (f32[2,8,128]{2,1,0:T(8,128)S(1)}, f32[2,8,128]{2,1,0:T(8,128)S(1)}, u32[]{:S(2)}, u32[]{:S(2)}) collective-permute-start(f32[2,8,128]{2,1,0:T(8,128)S(1)} %get-tuple-element.69), channel_id=1, source_target_pairs={{8,0},{16,8},{24,16},{9,1},{17,9},{25,17},{10,2},{18,10},{26,18},{... | collective-permute-start | bytes 24584 | tf_op jit(solution)/shard_map/ppermute | solution.py:20
  42.9 6.2 %collective-permute-start.8 = (f32[68,2,128]{2,1,0:T(2,128)S(1)}, f32[68,2,128]{2,1,0:T(2,128)S(1)}, u32[]{:S(2)}, u32[]{:S(2)}) collective-permute-start(f32[68,2,128]{2,1,0:T(2,128)S(1)} %get-tuple-element.63), channel_id=1, source_target_pairs={{4,0},{5,1},{6,2},{7,3},{12,8},{13,9},{14,10},{15,11},{20,16},{21,... | collective-permute-start | bytes 208904 | tf_op jit(solution)/shard_map/ppermute | solution.py:20
  44.2 6.5 %collective-permute-start.9 = (f32[68,2,128]{2,1,0:T(2,128)S(1)}, f32[68,2,128]{2,1,0:T(2,128)S(1)}, u32[]{:S(2)}, u32[]{:S(2)}) collective-permute-start(f32[68,2,128]{2,1,0:T(2,128)S(1)} %get-tuple-element.62), channel_id=1, source_target_pairs={{0,4},{1,5},{2,6},{3,7},{8,12},{9,13},{10,14},{11,15},{16,20},{17,... | collective-permute-start | bytes 208904 | tf_op jit(solution)/shard_map/ppermute | solution.py:19
  53.9 8.3 %collective-permute-start.10 = (f32[68,12,2]{0,2,1:T(2,128)S(1)}, f32[68,12,2]{0,2,1:T(2,128)S(1)}, u32[]{:S(2)}, u32[]{:S(2)}) collective-permute-start(f32[68,12,2]{0,2,1:T(2,128)S(1)} %copy.128), channel_id=1, source_target_pairs={{1,0},{2,1},{3,2},{5,4},{6,5},{7,6},{9,8},{10,9},{11,10},{13,12},{... | collective-permute-start | bytes 19592 | tf_op jit(solution)/shard_map/ppermute | solution.py:20
  57.1 6.3 %collective-permute-start.11 = (f32[68,12,2]{0,2,1:T(2,128)}, f32[68,12,2]{0,2,1:T(2,128)}, u32[]{:S(2)}, u32[]{:S(2)}) collective-permute-start(f32[68,12,2]{0,2,1:T(2,128)} %copy.130), channel_id=1, source_target_pairs={{0,1},{1,2},{2,3},{4,5},{5,6},{6,7},{8,9},{9,10},{10,11},{12,13},{... | collective-permute-start | bytes 19592 | tf_op jit(solution)/shard_map/ppermute | solution.py:19
  67.2 4.3 %collective-permute-start.12 = (f32[2,8,128]{2,1,0:T(8,128)S(1)}, f32[2,8,128]{2,1,0:T(8,128)S(1)}, u32[]{:S(2)}, u32[]{:S(2)}) collective-permute-start(f32[2,8,128]{2,1,0:T(8,128)S(1)} %get-tuple-element.67), channel_id=1, source_target_pairs={{8,0},{16,8},{24,16},{9,1},{17,9},{25,17},{10,2},{18,10},{26,18},{... | collective-permute-start | bytes 24584 | tf_op jit(solution)/shard_map/ppermute | solution.py:20
  72.4 6.2 %collective-permute-start.14 = (f32[68,2,128]{2,1,0:T(2,128)S(1)}, f32[68,2,128]{2,1,0:T(2,128)S(1)}, u32[]{:S(2)}, u32[]{:S(2)}) collective-permute-start(f32[68,2,128]{2,1,0:T(2,128)S(1)} %get-tuple-element.61), channel_id=1, source_target_pairs={{4,0},{5,1},{6,2},{7,3},{12,8},{13,9},{14,10},{15,11},{20,16},{21,... | collective-permute-start | bytes 208904 | tf_op jit(solution)/shard_map/ppermute | solution.py:20
  73.7 6.5 %collective-permute-start.15 = (f32[68,2,128]{2,1,0:T(2,128)S(1)}, f32[68,2,128]{2,1,0:T(2,128)S(1)}, u32[]{:S(2)}, u32[]{:S(2)}) collective-permute-start(f32[68,2,128]{2,1,0:T(2,128)S(1)} %get-tuple-element.60), channel_id=1, source_target_pairs={{0,4},{1,5},{2,6},{3,7},{8,12},{9,13},{10,14},{11,15},{16,20},{17,... | collective-permute-start | bytes 208904 | tf_op jit(solution)/shard_map/ppermute | solution.py:19
  83.3 7.4 %collective-permute-start.16 = (f32[68,12,2]{0,2,1:T(2,128)S(1)}, f32[68,12,2]{0,2,1:T(2,128)S(1)}, u32[]{:S(2)}, u32[]{:S(2)}) collective-permute-start(f32[68,12,2]{0,2,1:T(2,128)S(1)} %copy.132), channel_id=1, source_target_pairs={{1,0},{2,1},{3,2},{5,4},{6,5},{7,6},{9,8},{10,9},{11,10},{13,12},{... | collective-permute-start | bytes 19592 | tf_op jit(solution)/shard_map/ppermute | solution.py:20
  85.9 6.2 %collective-permute-start.17 = (f32[68,12,2]{0,2,1:T(2,128)S(1)}, f32[68,12,2]{0,2,1:T(2,128)S(1)}, u32[]{:S(2)}, u32[]{:S(2)}) collective-permute-start(f32[68,12,2]{0,2,1:T(2,128)S(1)} %copy.134), channel_id=1, source_target_pairs={{0,1},{1,2},{2,3},{4,5},{5,6},{6,7},{8,9},{9,10},{10,11},{12,13},{... | collective-permute-start | bytes 19592 | tf_op jit(solution)/shard_map/ppermute | solution.py:19
  95.9 5.2 %collective-permute-start.18 = (f32[2,8,128]{2,1,0:T(8,128)S(1)}, f32[2,8,128]{2,1,0:T(8,128)S(1)}, u32[]{:S(2)}, u32[]{:S(2)}) collective-permute-start(f32[2,8,128]{2,1,0:T(8,128)S(1)} %get-tuple-element.64), channel_id=1, source_target_pairs={{0,8},{8,16},{16,24},{1,9},{9,17},{17,25},{2,10},{10,18},{18,26},{... | collective-permute-start | bytes 24584 | tf_op jit(solution)/shard_map/ppermute | solution.py:19
  99.8 6.5 %collective-permute-start.19 = (f32[2,8,128]{2,1,0:T(8,128)S(1)}, f32[2,8,128]{2,1,0:T(8,128)S(1)}, u32[]{:S(2)}, u32[]{:S(2)}) collective-permute-start(f32[2,8,128]{2,1,0:T(8,128)S(1)} %get-tuple-element.65), channel_id=1, source_target_pairs={{8,0},{16,8},{24,16},{9,1},{17,9},{25,17},{10,2},{18,10},{26,18},{... | collective-permute-start | bytes 24584 | tf_op jit(solution)/shard_map/ppermute | solution.py:20
  106.3 6.2 %collective-permute-start.20 = (f32[68,2,128]{2,1,0:T(2,128)S(1)}, f32[68,2,128]{2,1,0:T(2,128)S(1)}, u32[]{:S(2)}, u32[]{:S(2)}) collective-permute-start(f32[68,2,128]{2,1,0:T(2,128)S(1)} %get-tuple-element.58), channel_id=1, source_target_pairs={{0,4},{1,5},{2,6},{3,7},{8,12},{9,13},{10,14},{11,15},{16,20},{17,... | collective-permute-start | bytes 208904 | tf_op jit(solution)/shard_map/ppermute | solution.py:19
  110.6 6.2 %collective-permute-start.21 = (f32[68,2,128]{2,1,0:T(2,128)S(1)}, f32[68,2,128]{2,1,0:T(2,128)S(1)}, u32[]{:S(2)}, u32[]{:S(2)}) collective-permute-start(f32[68,2,128]{2,1,0:T(2,128)S(1)} %get-tuple-element.59), channel_id=1, source_target_pairs={{4,0},{5,1},{6,2},{7,3},{12,8},{13,9},{14,10},{15,11},{20,16},{21,... | collective-permute-start | bytes 208904 | tf_op jit(solution)/shard_map/ppermute | solution.py:20
  120.0 7.5 %collective-permute-start.22 = (f32[68,12,2]{0,2,1:T(2,128)S(1)}, f32[68,12,2]{0,2,1:T(2,128)S(1)}, u32[]{:S(2)}, u32[]{:S(2)}) collective-permute-start(f32[68,12,2]{0,2,1:T(2,128)S(1)} %copy.136), channel_id=1, source_target_pairs={{0,1},{1,2},{2,3},{4,5},{5,6},{6,7},{8,9},{9,10},{10,11},{12,13},{... | collective-permute-start | bytes 19592 | tf_op jit(solution)/shard_map/ppermute | solution.py:19
  126.0 6.0 %collective-permute-start.23 = (f32[68,12,2]{0,2,1:T(2,128)}, f32[68,12,2]{0,2,1:T(2,128)}, u32[]{:S(2)}, u32[]{:S(2)}) collective-permute-start(f32[68,12,2]{0,2,1:T(2,128)} %copy.137), channel_id=1, source_target_pairs={{1,0},{2,1},{3,2},{5,4},{6,5},{7,6},{9,8},{10,9},{11,10},{13,12},{... | collective-permute-start | bytes 19592 | tf_op jit(solution)/shard_map/ppermute | solution.py:20
  142.0 10.6 %all-to-all-start = ((bf16[3,64,8,128]{3,2,0,1:T(8,128)(2,1)}), bf16[3,64,8,128]{3,2,0,1:T(8,128)(2,1)S(1)}, u32[]{:S(2)}, u32[]{:S(2)}) async-start(bf16[3,64,8,128]{3,2,0,1:T(8,128)(2,1)} %copy.142), calls=%async_computation | async-start | bytes 786432 | tf_op jit(solution)/shard_map/all_to_all | solution.py:161
  154.9 5.7 %collective-permute-start.25 = (f32[3,1,16,128]{3,2,1,0:T(8,128)S(1)}, f32[3,1,16,128]{3,2,1,0:T(8,128)S(1)}, u32[]{:S(2)}, u32[]{:S(2)}) collective-permute-start(f32[3,1,16,128]{3,2,1,0:T(8,128)S(1)} %get-tuple-element.47), channel_id=1, source_target_pairs={{4,0},{8,4},{12,8},{16,12},{20,16},{24,20},{28,24},{5,1},{9,5},{13... | collective-permute-start | bytes 73736 | tf_op jit(solution)/shard_map/ppermute | solution.py:20
  161.5 5.0 %collective-permute-start.26 = (f32[3,34,16,1]{1,2,3,0:T(8,128)S(1)}, f32[3,34,16,1]{1,2,3,0:T(8,128)S(1)}, u32[]{:S(2)}, u32[]{:S(2)}) collective-permute-start(f32[3,34,16,1]{1,2,3,0:T(8,128)S(1)} %copy.157), channel_id=1, source_target_pairs={{0,1},{1,2},{2,3},{4,5},{5,6},{6,7},{8,9},{9,10},{10,11},{12,13},{... | collective-permute-start | bytes 19592 | tf_op jit(solution)/shard_map/ppermute | solution.py:19
  165.2 5.7 %collective-permute-start.27 = (f32[3,34,16,1]{1,2,3,0:T(8,128)S(1)}, f32[3,34,16,1]{1,2,3,0:T(8,128)S(1)}, u32[]{:S(2)}, u32[]{:S(2)}) collective-permute-start(f32[3,34,16,1]{1,2,3,0:T(8,128)S(1)} %copy.158), channel_id=1, source_target_pairs={{1,0},{2,1},{3,2},{5,4},{6,5},{7,6},{9,8},{10,9},{11,10},{13,12},{... | collective-permute-start | bytes 19592 | tf_op jit(solution)/shard_map/ppermute | solution.py:20
  177.9 5.7 %collective-permute-start.29 = (f32[3,1,16,128]{3,2,1,0:T(8,128)S(1)}, f32[3,1,16,128]{3,2,1,0:T(8,128)S(1)}, u32[]{:S(2)}, u32[]{:S(2)}) collective-permute-start(f32[3,1,16,128]{3,2,1,0:T(8,128)S(1)} %get-tuple-element.45), channel_id=1, source_target_pairs={{4,0},{8,4},{12,8},{16,12},{20,16},{24,20},{28,24},{5,1},{9,5},{13... | collective-permute-start | bytes 73736 | tf_op jit(solution)/shard_map/ppermute | solution.py:20
  184.4 5.2 %collective-permute-start.30 = (f32[3,34,16,1]{1,2,3,0:T(8,128)S(1)}, f32[3,34,16,1]{1,2,3,0:T(8,128)S(1)}, u32[]{:S(2)}, u32[]{:S(2)}) collective-permute-start(f32[3,34,16,1]{1,2,3,0:T(8,128)S(1)} %copy.159), channel_id=1, source_target_pairs={{0,1},{1,2},{2,3},{4,5},{5,6},{6,7},{8,9},{9,10},{10,11},{12,13},{... | collective-permute-start | bytes 19592 | tf_op jit(solution)/shard_map/ppermute | solution.py:19
  188.3 5.7 %collective-permute-start.31 = (f32[3,34,16,1]{1,2,3,0:T(8,128)S(1)}, f32[3,34,16,1]{1,2,3,0:T(8,128)S(1)}, u32[]{:S(2)}, u32[]{:S(2)}) collective-permute-start(f32[3,34,16,1]{1,2,3,0:T(8,128)S(1)} %copy.160), channel_id=1, source_target_pairs={{1,0},{2,1},{3,2},{5,4},{6,5},{7,6},{9,8},{10,9},{11,10},{13,12},{... | collective-permute-start | bytes 19592 | tf_op jit(solution)/shard_map/ppermute | solution.py:20
  199.1 4.6 %collective-permute-start.32 = (f32[3,1,16,128]{3,2,1,0:T(8,128)S(1)}, f32[3,1,16,128]{3,2,1,0:T(8,128)S(1)}, u32[]{:S(2)}, u32[]{:S(2)}) collective-permute-start(f32[3,1,16,128]{3,2,1,0:T(8,128)S(1)} %get-tuple-element.42), channel_id=1, source_target_pairs={{0,4},{4,8},{8,12},{12,16},{16,20},{20,24},{24,28},{1,5},{5,9},{9,... | collective-permute-start | bytes 73736 | tf_op jit(solution)/shard_map/ppermute | solution.py:19
  202.2 5.9 %collective-permute-start.33 = (f32[3,1,16,128]{3,2,1,0:T(8,128)S(1)}, f32[3,1,16,128]{3,2,1,0:T(8,128)S(1)}, u32[]{:S(2)}, u32[]{:S(2)}) collective-permute-start(f32[3,1,16,128]{3,2,1,0:T(8,128)S(1)} %get-tuple-element.43), channel_id=1, source_target_pairs={{4,0},{8,4},{12,8},{16,12},{20,16},{24,20},{28,24},{5,1},{9,5},{13... | collective-permute-start | bytes 73736 | tf_op jit(solution)/shard_map/ppermute | solution.py:20
  208.9 3.9 %collective-permute-start.34 = (f32[3,34,16,1]{1,2,3,0:T(8,128)S(1)}, f32[3,34,16,1]{1,2,3,0:T(8,128)S(1)}, u32[]{:S(2)}, u32[]{:S(2)}) collective-permute-start(f32[3,34,16,1]{1,2,3,0:T(8,128)S(1)} %copy.161), channel_id=1, source_target_pairs={{0,1},{1,2},{2,3},{4,5},{5,6},{6,7},{8,9},{9,10},{10,11},{12,13},{... | collective-permute-start | bytes 19592 | tf_op jit(solution)/shard_map/ppermute | solution.py:19
  211.6 5.7 %collective-permute-start.35 = (f32[3,34,16,1]{1,2,3,0:T(8,128)S(1)}, f32[3,34,16,1]{1,2,3,0:T(8,128)S(1)}, u32[]{:S(2)}, u32[]{:S(2)}) collective-permute-start(f32[3,34,16,1]{1,2,3,0:T(8,128)S(1)} %copy.162), channel_id=1, source_target_pairs={{1,0},{2,1},{3,2},{5,4},{6,5},{7,6},{9,8},{10,9},{11,10},{13,12},{... | collective-permute-start | bytes 19592 | tf_op jit(solution)/shard_map/ppermute | solution.py:20
  (26 other events, 80.5 us)
